TPU v7x, 128 devices: a whole 4x4x4 slice. The times are simulated.
128 devices in a mesh: gx: 8 (over z, core), gy: 16 (over y, x).
Axes of the slice: x: 4, y: 4, z: 4, core: 2. Of those that a mesh axis runs over, the one named last changes fastest.
Arguments:
- displacement: float32 [3, 24, 384, 384], P(None, 'gx', 'gy'), may hold values from -1.6015 to 1.6015, as said below
- velocity: float32 [3, 24, 384, 384], P(None, 'gx', 'gy'), may hold values from -6 to 6
- energy: float32 [27, 8, 128, 128], P(None, 'gx', 'gy'), may hold values from 0.5 to 18
- mass_weight: float32 [216, 8, 128, 128], P(None, 'gx', 'gy'), may hold values from 0.002 to 0.02
- pinned_flags: int32 [3, 24, 384, 384], P(None, 'gx', 'gy'), may hold values 0 or 1
Outputs:
- acceleration: float32 [3, 24, 384, 384], P(None, 'gx', 'gy')
- velocity_new: float32 [3, 24, 384, 384], P(None, 'gx', 'gy')
- displacement_new: float32 [3, 24, 384, 384], P(None, 'gx', 'gy')
- energy_new: float32 [27, 8, 128, 128], P(None, 'gx', 'gy')
Inputs may be any that keep to these rules, and one draw needn't show every extreme that they name: Every entry of the displacement's derivative along local element coordinates stays below 0.11 in magnitude.
All inputs are finite; a program needn't handle non-finite values. No bound on the sum of `pinned_flags` on one device may be relied on, other than what follows from the above.
Results may differ from a plain program's by a relative error of at most 0.00018.
Values sent between devices are 32-bit elements; how exact they have to be, the bound alone decides.
No kernel may reach another device: no remote copies, remote signals or barrier semaphores. Data moves between devices by JAX's collectives and lax.ppermute only.
A program may use at most 128 MiB of HBM per device.

v0:
```python
from functools import partial
import math
import jax
import jax.numpy as jnp
import numpy as np
from jax import lax
from jax.sharding import PartitionSpec as P

Q = 6
ITERS = 3
HIGHEST = lax.Precision.HIGHEST
step_size = 0.05
viscosity = 0.3
gamma_less = 0.4


def shifted_2(shard, axis, by):
    devices = lax.axis_size(axis)
    return lax.ppermute(shard, axis, [(i, (i + by) % devices) for i in range(devices)])


def basis_tables():
    root_five = 1.0 / math.sqrt(5.0)
    lobatto = np.array([0.0, 0.5 - 0.5 * root_five, 0.5 + 0.5 * root_five, 1.0])
    legendre = np.array(
        [
            -0.932469514203152,
            -0.6612093864662645,
            -0.2386191860831909,
            0.2386191860831909,
            0.6612093864662645,
            0.932469514203152,
        ]
    )
    abscissa = 0.5 + 0.5 * legendre
    shape_values = np.ones((6, 4))
    shape_slopes = np.zeros((6, 4))
    for a in range(4):
        for b in range(4):
            if b != a:
                shape_values[:, a] = (
                    shape_values[:, a] * (abscissa - lobatto[b]) / (lobatto[a] - lobatto[b])
                )
        for c in range(4):
            if c != a:
                factor_term = np.ones(6) / (lobatto[a] - lobatto[c])
                for b in range(4):
                    if b != a and b != c:
                        factor_term = (
                            factor_term * (abscissa - lobatto[b]) / (lobatto[a] - lobatto[b])
                        )
                shape_slopes[:, a] = shape_slopes[:, a] + factor_term
    thermo_values = np.stack(
        [
            (1.0 - abscissa) * (1.0 - abscissa),
            2.0 * abscissa * (1.0 - abscissa),
            abscissa * abscissa,
        ],
        axis=1,
    )
    return (
        jnp.asarray(shape_values, jnp.float32),
        jnp.asarray(shape_slopes, jnp.float32),
        jnp.asarray(thermo_values, jnp.float32),
    )


def along_x(matrix, operand):
    return jnp.einsum("qa,cabgjk->cqbgjk", matrix, operand, precision=HIGHEST)


def along_y(matrix, operand):
    return jnp.einsum("qb,cabgjk->caqgjk", matrix, operand, precision=HIGHEST)


def along_z(matrix, operand):
    return jnp.einsum("qg,cabgjk->cabqjk", matrix, operand, precision=HIGHEST)


def split_nodes(operand, which_axis):
    num_cells = (operand.shape[which_axis] - 1) // 3
    outer_dims = operand.shape[:which_axis]
    inner_dims = operand.shape[which_axis + 1 :]
    head_part = lax.slice_in_dim(operand, 0, 3 * num_cells, axis=which_axis).reshape(
        outer_dims + (num_cells, 3) + inner_dims
    )
    head_part = jnp.moveaxis(head_part, which_axis + 1, which_axis)
    tail_part = lax.slice_in_dim(operand, 3, 3 * num_cells + 1, stride=3, axis=which_axis)
    return jnp.concatenate([head_part, jnp.expand_dims(tail_part, which_axis)], axis=which_axis)


def merge_nodes(operand, which_axis):
    num_cells = operand.shape[which_axis + 1]
    outer_dims = operand.shape[:which_axis]
    inner_dims = operand.shape[which_axis + 2 :]
    head_part = jnp.moveaxis(
        lax.slice_in_dim(operand, 0, 3, axis=which_axis), which_axis, which_axis + 1
    )
    head_part = head_part.reshape(outer_dims + (3 * num_cells,) + inner_dims)
    tail_part = jnp.moveaxis(
        lax.slice_in_dim(operand, 3, 4, axis=which_axis), which_axis, which_axis + 1
    )
    pad_tail = [(0, 0)] * tail_part.ndim
    pad_tail[which_axis + 1] = (0, 2)
    tail_part = jnp.pad(tail_part, pad_tail).reshape(outer_dims + (3 * num_cells,) + inner_dims)
    pad_head = [(0, 0)] * head_part.ndim
    pad_head[which_axis] = (0, 1)
    pad_shift = [(0, 0)] * head_part.ndim
    pad_shift[which_axis] = (3, 0)
    shifted = lax.slice_in_dim(jnp.pad(tail_part, pad_shift), 0, 3 * num_cells + 1, axis=which_axis)
    return jnp.pad(head_part, pad_head) + shifted


def slab_elements(slab_field):
    closed = jnp.concatenate([slab_field, slab_field[..., :1]], axis=-1)
    parts_y = split_nodes(closed, 2)
    parts_z = split_nodes(parts_y, 4)
    return jnp.moveaxis(parts_z, 4, 3)


def slab_assemble(element_field):
    parts_z = merge_nodes(jnp.moveaxis(element_field, 3, 4), 4)
    parts_y = merge_nodes(parts_z, 2)
    return jnp.concatenate([parts_y[..., :1] + parts_y[..., -1:], parts_y[..., 1:-1]], axis=-1)


def over_blocks(node_fields, cell_data, element_fn):
    num_cells = cell_data[0].shape[1]

    def one_block(block_index):
        node_start = 3 * block_index
        element_sets = tuple(
            (
                slab_elements(lax.dynamic_slice_in_dim(field_in, node_start, 4, axis=1))
                for field_in in node_fields
            )
        )
        cell_block = tuple(
            (
                lax.dynamic_index_in_dim(member, block_index, axis=1, keepdims=False)
                for member in cell_data
            )
        )
        contribution, outputs_extra = element_fn(element_sets, cell_block)
        return (slab_assemble(contribution), outputs_extra)

    node_pieces, extra_parts = lax.map(one_block, jnp.arange(num_cells, dtype=jnp.int32))
    assembled = merge_nodes(jnp.moveaxis(node_pieces, 0, 2), 1)
    return (assembled, tuple((jnp.moveaxis(member, 0, 1) for member in extra_parts)))


def thermo_interp(thermo_values, dofs):
    return along_x(thermo_values, along_y(thermo_values, along_z(thermo_values, dofs[None])))[0]


def thermo_project(thermo_values, at_quad):
    moved = thermo_values.T
    return along_x(moved, along_y(moved, along_z(moved, at_quad[None])))[0]


def force_block(element_sets, cell_block, basis_set):
    shape_values, shape_slopes, thermo_values = basis_set
    kinematic = element_sets[0]
    energy_block, weight_block = cell_block
    trailing_shape = energy_block.shape[1:]
    z_values = along_z(shape_values, kinematic)
    z_slopes = along_z(shape_slopes, kinematic)
    yz_values = along_y(shape_values, z_values)
    gradients = [
        along_x(shape_slopes, yz_values),
        along_x(shape_values, along_y(shape_slopes, z_values)),
        along_x(shape_values, along_y(shape_values, z_slopes)),
    ]
    jacobian = [[gradients[d][c] + (1.0 if c == d else 0.0) for d in range(3)] for c in range(3)]
    grad_vel = [[gradients[d][3 + c] for d in range(3)] for c in range(3)]
    cofactor = [
        [
            jacobian[(c + 1) % 3][(d + 1) % 3] * jacobian[(c + 2) % 3][(d + 2) % 3]
            - jacobian[(c + 1) % 3][(d + 2) % 3] * jacobian[(c + 2) % 3][(d + 1) % 3]
            for d in range(3)
        ]
        for c in range(3)
    ]
    determinant = (
        jacobian[0][0] * cofactor[0][0]
        + jacobian[0][1] * cofactor[0][1]
        + jacobian[0][2] * cofactor[0][2]
    )
    inverse_det = 1.0 / determinant
    spatial_grad = [
        [
            (
                grad_vel[c][0] * cofactor[e][0]
                + grad_vel[c][1] * cofactor[e][1]
                + grad_vel[c][2] * cofactor[e][2]
            )
            * inverse_det
            for e in range(3)
        ]
        for c in range(3)
    ]
    energy_quad = thermo_interp(thermo_values, energy_block.reshape((3, 3, 3) + trailing_shape))
    mass_quad = weight_block.reshape((Q, Q, Q) + trailing_shape)
    scale_quad = mass_quad * inverse_det
    stress_shape = [
        [
            viscosity * (spatial_grad[c][d] + spatial_grad[d][c])
            - (gamma_less * energy_quad if c == d else 0.0)
            for d in range(3)
        ]
        for c in range(3)
    ]
    flux = [
        [
            scale_quad
            * (
                stress_shape[c][0] * cofactor[0][f]
                + stress_shape[c][1] * cofactor[1][f]
                + stress_shape[c][2] * cofactor[2][f]
            )
            for f in range(3)
        ]
        for c in range(3)
    ]
    power_quad = jnp.zeros_like(mass_quad)
    for c in range(3):
        for f in range(3):
            power_quad = power_quad + flux[c][f] * grad_vel[c][f]
    flux_cols = [jnp.stack([flux[c][f] for c in range(3)]) for f in range(3)]
    moved = along_x(shape_slopes.T, along_y(shape_values.T, along_z(shape_values.T, flux_cols[0])))
    moved = moved + along_x(
        shape_values.T,
        along_y(shape_slopes.T, along_z(shape_values.T, flux_cols[1]))
        + along_y(shape_values.T, along_z(shape_slopes.T, flux_cols[2])),
    )
    energy_rhs = thermo_project(thermo_values, power_quad)
    lumped_mass = thermo_project(thermo_values, mass_quad)
    energy_next = energy_block + step_size * (energy_rhs / lumped_mass).reshape(energy_block.shape)
    return (-moved, (energy_next,))


def mass_block(element_sets, cell_block, basis_set):
    shape_values = basis_set[0]
    mass_quad = cell_block[0].reshape((Q, Q, Q) + cell_block[0].shape[1:])
    at_quad = (
        along_x(shape_values, along_y(shape_values, along_z(shape_values, element_sets[0])))
        * mass_quad
    )
    return (along_x(shape_values.T, along_y(shape_values.T, along_z(shape_values.T, at_quad))), ())


def extend_right(field_in):
    right_rim = shifted_2(field_in[:, :1], "gx", -1)
    wide_field = jnp.concatenate([field_in, right_rim], axis=1)
    top_rim = shifted_2(wide_field[:, :, :1], "gy", -1)
    return jnp.concatenate([wide_field, top_rim], axis=2)


def fold_back(field_in):
    upper_rim = shifted_2(field_in[:, :, -1:], "gy", 1)
    field_in = jnp.concatenate([field_in[:, :, :1] + upper_rim, field_in[:, :, 1:-1]], axis=2)
    side_rim = shifted_2(field_in[:, -1:], "gx", 1)
    return jnp.concatenate([field_in[:, :1] + side_rim, field_in[:, 1:-1]], axis=1)


def global_sum(value):
    return lax.psum(value, ("gx", "gy"))


def on_device(displacement, velocity, energy, mass_weight, pinned_flags):
    basis_set = basis_tables()
    free_mask = (1 - pinned_flags).astype(jnp.float32)
    kinematic = jnp.concatenate([displacement, velocity], axis=0)
    mass_apply = partial(mass_block, basis_set=basis_set)
    rows_x = displacement.shape[1]
    rows_y = displacement.shape[2]
    assembled, extra_parts = over_blocks(
        (extend_right(kinematic),), (energy, mass_weight), partial(force_block, basis_set=basis_set)
    )
    nodal_force = fold_back(assembled)
    owned = 1.0
    residual = free_mask * nodal_force
    energy_new = extra_parts[0]

    def local_inner(first, second):
        return jnp.sum(owned * (first * second))

    acceleration = jnp.zeros_like(residual)
    direction = residual
    norm_now = global_sum(local_inner(residual, residual))
    for iteration in range(ITERS):
        contribution = over_blocks((extend_right(direction),), (mass_weight,), mass_apply)[0]
        mass_image = free_mask * fold_back(contribution)
        step_length = norm_now / global_sum(local_inner(direction, mass_image))
        acceleration = acceleration + step_length * direction
        residual = residual - step_length * mass_image
        norm_next = global_sum(local_inner(residual, residual))
        direction = residual + norm_next / norm_now * direction
        norm_now = norm_next
    acceleration = acceleration[:, :rows_x, :rows_y]
    velocity_new = velocity + step_size * acceleration
    displacement_new = displacement + step_size * velocity_new
    return (acceleration, velocity_new, displacement_new, energy_new)


def solution(mesh):
    in_specs = (
        P(None, "gx", "gy", None),
        P(None, "gx", "gy", None),
        P(None, "gx", "gy", None),
        P(None, "gx", "gy", None),
        P(None, "gx", "gy", None),
    )
    out_specs = (
        P(None, "gx", "gy", None),
        P(None, "gx", "gy", None),
        P(None, "gx", "gy", None),
        P(None, "gx", "gy", None),
    )
    return jax.shard_map(
        on_device, mesh=mesh, in_specs=in_specs, out_specs=out_specs, check_vma=False
    )
```

profile of v0, /device:TPU:1, one launch (start us, length us, event | category | flops | bytes accessed | tf_op | source)
XLA Modules:
  0.0 1001.1 jit_solution(13770269630577380290)
XLA Ops:
  21.4 12.5 %copy.282 = f32[6,4,4,8,384]{3,2,4,1,0:T(4,128)} copy(f32[6,4,4,8,384]{4,3,2,1,0:T(8,128)S(1)} %fusion.109) | data formatting | bytes 2359296 | tf_op jit(solution)/shard_map/while/body/eval_jaxpr/slice | solution.py:84
  33.9 18.3 %copy.283 = f32[6,4,4,8,128,3]{4,5,3,2,1,0:T(4,128)S(1)} copy(f32[6,4,4,8,128,3]{3,2,5,4,1,0:T(4,128)} %bitcast.311) | data formatting | bytes 2359296 | tf_op jit(solution)/shard_map/while/body/eval_jaxpr/reshape | solution.py:84
  52.2 15.2 %slice.434 = f32[6,4,4,8,128]{4,3,2,1,0:T(8,128)S(1)} slice(f32[6,4,4,8,385]{4,3,2,1,0:T(8,128)} %pad_maximum_fusion.3), slice={[0:6:1], [0:4:1], [0:4:1], [0:8:1], [3:385:3]} | slice | bytes 786432 | tf_op jit(solution)/shard_map/while/body/eval_jaxpr/slice | solution.py:88
  86.1 9.3 fusion.18
  101.1 9.5 fusion.16
  110.6 9.5 fusion.20
  121.0 10.7 %copy_bitcast_fusion = (f32[6,6,6,6,8,128]{5,4,3,2,1,0:T(8,128)}, f32[6,6,6,6,8,128]{5,4,3,2,1,0:T(8,128)}) fusion(f32[6,6,6,8,128,6]{4,5,3,2,1,0:T(8,128)} %fusion.16, f32[6,6,6,8,128,6]{4,5,3,2,1,0:T(8,128)} %fusion.18), kind=kLoop, calls=%fused_computation.12 | loop fusion | bytes 21233664 | tf_op jit(solution)/shard_map/while/body/eval_jaxpr/qa,cabgjk->cqbgjk/transpose | solution.py:69
  144.5 11.0 %add_bitcast_fusion = (f32[6,6,6,8,128]{4,3,2,1,0:T(8,128)}, f32[1,6,6,6,8,128]{5,4,3,2,1,0:T(8,128)}, f32[1,6,6,6,8,128]{5,4,3,2,1,0:T(8,128)}, f32[1,6,6,6,8,1...) fusion(f32[1,6,6,6,8,128]{5,4,3,2,1,0:T(8,128)S(1)} %get-tuple-, ...), kind=kLoop, calls=%fused_computation.143 | loop fusion | flops 25878528 | bytes 31850496 | tf_op jit(solution)/shard_map/reshape.83
  198.9 10.8 %fusion = f32[3,4,4,8,385]{3,2,4,1,0:T(4,128)} fusion(f32[3,4,4,8,384]{3,2,4,1,0:T(4,128)} %bitcast.323, f32[3,4,4,8,384]{3,2,4,1,0:T(4,128)S(1)} %bitcast.319), kind=kLoop, calls=%fused_computation.4 | loop fusion | flops 147840 | bytes 1771008 | tf_op jit(solution)/shard_map/while/body/eval_jaxpr/add | solution.py:111
  223.7 9.2 copy.307
  270.3 10.3 %copy.315 = f32[3,4,4,8,128,3]{4,5,3,2,1,0:T(4,128)} copy(f32[3,4,4,8,128,3]{3,2,5,4,1,0:T(4,128)} %bitcast.327) | data formatting | bytes 1179648 | tf_op jit(solution)/shard_map/while/body/eval_jaxpr/reshape | solution.py:84
  328.2 12.8 %fusion.1 = f32[3,4,4,8,385]{3,2,4,1,0:T(4,128)} fusion(f32[3,4,4,8,384]{3,2,4,1,0:T(4,128)} %bitcast.320, f32[3,4,4,8,384]{3,2,4,1,0:T(4,128)} %bitcast.324), kind=kLoop, calls=%fused_computation.5 | loop fusion | flops 147840 | bytes 1771008 | tf_op jit(solution)/shard_map/while/body/eval_jaxpr/add | solution.py:111
  356.5 10.0 copy.324
  388.2 66.0 %all-reduce.36 = (f32[]{:T(128)}, f32[]{:T(128)}) all-reduce(f32[]{:T(128)} %get-tuple-element.88, f32[]{:T(128)} %get-tuple-element.87), channel_id=1, replica_groups=mesh['gx'=8,'gy'=16] {'gx','gy'}, use_global_device_ids=true, to_apply=%region_1.2 | all-reduce | flops 2 | bytes 16 | tf_op jit(solution)/shard_map/psum | solution.py:267
  457.2 62.5 %psum.44 = f32[]{:T(128)} all-reduce(f32[]{:T(128)} %get-tuple-element.114), channel_id=1, replica_groups=mesh['gx'=8,'gy'=16] {'gx','gy'}, use_global_device_ids=true, to_apply=%region_5.6 | all-reduce | flops 1 | bytes 8 | tf_op jit(solution)/shard_map/psum | solution.py:267
  544.6 10.3 %copy.333 = f32[3,4,4,8,128,3]{4,5,3,2,1,0:T(4,128)} copy(f32[3,4,4,8,128,3]{3,2,5,4,1,0:T(4,128)} %bitcast.328) | data formatting | bytes 1179648 | tf_op jit(solution)/shard_map/while/body/eval_jaxpr/reshape | solution.py:84
  605.0 12.8 %fusion.2 = f32[3,4,4,8,385]{3,2,4,1,0:T(4,128)} fusion(f32[3,4,4,8,384]{3,2,4,1,0:T(4,128)} %bitcast.321, f32[3,4,4,8,384]{3,2,4,1,0:T(4,128)} %bitcast.325), kind=kLoop, calls=%fused_computation.6 | loop fusion | flops 147840 | bytes 1771008 | tf_op jit(solution)/shard_map/while/body/eval_jaxpr/add | solution.py:111
  633.3 10.0 copy.341
  665.9 65.0 %psum.45 = f32[]{:T(128)} all-reduce(f32[]{:T(128)} %get-tuple-element.112), channel_id=1, replica_groups=mesh['gx'=8,'gy'=16] {'gx','gy'}, use_global_device_ids=true, to_apply=%region_7.8 | all-reduce | flops 1 | bytes 8 | tf_op jit(solution)/shard_map/psum | solution.py:267
  735.6 62.5 %psum.46 = f32[]{:T(128)} all-reduce(f32[]{:T(128)} %multiply_reduce_fusion), channel_id=1, replica_groups=mesh['gx'=8,'gy'=16] {'gx','gy'}, use_global_device_ids=true, to_apply=%region_9.10 | all-reduce | flops 1 | bytes 8 | tf_op jit(solution)/shard_map/psum | solution.py:267
  821.2 10.3 %copy.350 = f32[3,4,4,8,128,3]{4,5,3,2,1,0:T(4,128)} copy(f32[3,4,4,8,128,3]{3,2,5,4,1,0:T(4,128)} %bitcast.329) | data formatting | bytes 1179648 | tf_op jit(solution)/shard_map/while/body/eval_jaxpr/reshape | solution.py:84
  877.1 12.9 %fusion.3 = f32[3,4,4,8,385]{3,2,4,1,0:T(4,128)} fusion(f32[3,4,4,8,384]{3,2,4,1,0:T(4,128)} %bitcast.322, f32[3,4,4,8,384]{3,2,4,1,0:T(4,128)} %bitcast.326), kind=kLoop, calls=%fused_computation.7 | loop fusion | flops 147840 | bytes 1771008 | tf_op jit(solution)/shard_map/while/body/eval_jaxpr/add | solution.py:111
  905.4 9.1 copy.358
  933.3 65.1 %psum.47 = f32[]{:T(128)} all-reduce(f32[]{:T(128)} %fusion.140), channel_id=1, replica_groups=mesh['gx'=8,'gy'=16] {'gx','gy'}, use_global_device_ids=true, to_apply=%region_11.12 | all-reduce | flops 1 | bytes 8 | tf_op jit(solution)/shard_map/psum | solution.py:267
  (293 shorter events, 456.6 us)
Async XLA Ops:
  0.6 13.7 %copy-start.25 = (f32[6,3,1,1,1]{0,1,4,3,2:T(4,128)S(1)}, f32[6,3,1,1,1]{0,1,4,3,2:T(4,128)}, u32[]{:S(2)}) copy-start(f32[6,3,1,1,1]{0,1,4,3,2:T(4,128)} %constant.174) | copy-start | bytes 220
  2.7 6.7 collective-permute-start
  9.4 6.4 collective-permute-start.1
  33.9 33.5 %copy-start.18 = (f32[6,4,1,1,1,1]{0,1,5,4,3,2:T(4,128)S(1)}, f32[6,4,1,1,1,1]{0,1,5,4,3,2:T(4,128)}, u32[]{:S(2)}) copy-start(f32[6,4,1,1,1,1]{0,1,5,4,3,2:T(4,128)} %constant.172) | copy-start | bytes 292
  235.7 10.8 %copy-start.3 = (s32[3,3,24,384]{3,2,1,0:T(8,128)S(1)}, s32[3,3,24,384]{3,2,1,0:T(8,128)}, u32[]{:S(2)}) copy-start(s32[3,3,24,384]{3,2,1,0:T(8,128)} %param.12) | copy-start | bytes 995332
  235.8 18.2 %copy-start.2 = (f32[216,1,8,128]{3,2,1,0:T(8,128)S(1)}, f32[216,1,8,128]{3,2,1,0:T(8,128)}, u32[]{:S(2)}) copy-start(f32[216,1,8,128]{3,2,1,0:T(8,128)} %param.11) | copy-start | bytes 2654212
  235.8 6.0 collective-permute-start.2
  241.9 4.6 collective-permute-start.3
  246.6 5.5 collective-permute-start.4
  252.2 2.7 collective-permute-start.5
  376.8 6.3 collective-permute-start.6
  383.1 4.2 collective-permute-start.7
  387.4 66.8 %copy-start.22 = (f32[3,1,24,384]{3,2,1,0:T(8,128)}, f32[3,1,24,384]{3,2,1,0:T(8,128)S(1)}, u32[]{:S(2)}) copy-start(f32[3,1,24,384]{3,2,1,0:T(8,128)S(1)} %maximum_add_fusion.2) | copy-start | bytes 331780
  521.1 4.2 collective-permute-start.8
  525.3 3.2 collective-permute-start.9
  654.9 6.7 collective-permute-start.10
  661.7 3.5 collective-permute-start.11
  799.5 4.2 collective-permute-start.12
  803.7 3.9 collective-permute-start.13
  922.4 6.0 collective-permute-start.14
  923.4 9.2 copy-start.23
  923.4 76.3 %copy-start.19 = (f32[3,3,24,384]{3,2,1,0:T(8,128)S(1)}, f32[3,3,24,384]{3,2,1,0:T(8,128)}, u32[]{:S(2)}) copy-start(f32[3,3,24,384]{3,2,1,0:T(8,128)} %param.8) | copy-start | bytes 995332
  923.4 76.3 %copy-start.20 = (f32[3,3,24,384]{3,2,1,0:T(8,128)S(1)}, f32[3,3,24,384]{3,2,1,0:T(8,128)}, u32[]{:S(2)}) copy-start(f32[3,3,24,384]{3,2,1,0:T(8,128)} %param.9) | copy-start | bytes 995332
  928.4 3.5 collective-permute-start.15
  (24 other events, 90.7 us)
where the time goes:
time: 1010 us; the launch traced here: 1000 us
  local copies, waits for them, and re-layouts  364 us (36%)
  blocking collectives  321 us (32%)
  matrix products  153 us (15%)
  other arithmetic  88.8 us (9%)
  waiting for transfers between devices  40 us (4%)
  starting transfers between devices  25.2 us (2%)
    psum x5, blocking collectives, global_sum(): return lax.psum(value, ('gx', 'gy'))  321 us
    transpose x16, local copies, waits for them, and re-layouts, merge_nodes(): jnp.moveaxis(lax.slice_in_dim(operand, 0, 3, axis=which_axis), which_axis...  104 us
    dot_general x14, matrix products, along_x(): return jnp.einsum('qa,cabgjk->cqbgjk', matrix, operand, precision=HIGHEST)  55.3 us
    dot_general x15, matrix products, along_y(): return jnp.einsum('qb,cabgjk->caqgjk', matrix, operand, precision=HIGHEST)  50.4 us
    reshape x8, local copies, waits for them, and re-layouts, split_nodes(): lax.slice_in_dim(operand, 0, 3 * num_cells, axis=which_axis)  50.1 us
    add x12, other arithmetic, merge_nodes(): return jnp.pad(head_part, pad_head) + shifted  50 us
    dot_general x14, matrix products, along_z(): return jnp.einsum('qg,cabgjk->cabqjk', matrix, operand, precision=HIGHEST)  47.1 us
    slice x8, local copies, waits for them, and re-layouts, split_nodes(): lax.slice_in_dim(operand, 3, 3 * num_cells + 1, stride=3, axis=which_axis)  46.5 us
  transfers between devices with their start and end apart: 16, of which 13 were waited for; matrix products, arithmetic and copies ran while one was open for 1% of the time, Pallas kernels for 0%

commit v1 on v0

--- a/solution.py
+++ b/solution.py
@@ -264,7 +264,7 @@
 
 
 def global_sum(value):
-    return lax.psum(value, ("gx", "gy"))
+    return lax.psum(lax.psum(value, "gy"), "gx")
 
 
 def on_device(displacement, velocity, energy, mass_weight, pinned_flags):

time: 1010 us -> 958 us (0.949)
  blocking collectives: 321 us -> 259 us
    psum x5 -> x10, blocking collectives: 321 us -> 259 us  [global_sum(): return lax.psum(lax.psum(value, 'gy'), 'gx')]
    unnamed x73 -> x81, local copies, waits for them, and re-layouts: 39.7 us -> 42.1 us
  transfers between devices with their start and end apart: 16 -> 16, of which waited for: 13 -> 14; matrix products, arithmetic and copies ran while one was open for 1% -> 1% of each run, Pallas kernels for 0% -> 0%
where the time goes in v1:
time: 958 us; the launch traced here: 946 us
  local copies, waits for them, and re-layouts  366 us (38%)
  blocking collectives  259 us (27%)
  matrix products  154 us (16%)
  other arithmetic  92.9 us (10%)
  waiting for transfers between devices  40.5 us (4%)
  starting transfers between devices  25.1 us (3%)
    psum x10, blocking collectives, global_sum(): return lax.psum(lax.psum(value, 'gy'), 'gx')  259 us
    transpose x16, local copies, waits for them, and re-layouts, merge_nodes(): jnp.moveaxis(lax.slice_in_dim(operand, 0, 3, axis=which_axis), which_axis...  102 us
    dot_general x14, matrix products, along_x(): return jnp.einsum('qa,cabgjk->cqbgjk', matrix, operand, precision=HIGHEST)  56.4 us
    dot_general x15, matrix products, along_y(): return jnp.einsum('qb,cabgjk->caqgjk', matrix, operand, precision=HIGHEST)  50.7 us
    reshape x8, local copies, waits for them, and re-layouts, split_nodes(): lax.slice_in_dim(operand, 0, 3 * num_cells, axis=which_axis)  50.1 us
    add x12, other arithmetic, merge_nodes(): return jnp.pad(head_part, pad_head) + shifted  49.9 us
    dot_general x14, matrix products, along_z(): return jnp.einsum('qg,cabgjk->cabqjk', matrix, operand, precision=HIGHEST)  47.3 us
    slice x8, local copies, waits for them, and re-layouts, split_nodes(): lax.slice_in_dim(operand, 3, 3 * num_cells + 1, stride=3, axis=which_axis)  46 us
  transfers between devices with their start and end apart: 16, of which 14 were waited for; matrix products, arithmetic and copies ran while one was open for 1% of the time, Pallas kernels for 0%

profile of v1, /device:TPU:1, one launch (start us, length us, event | category | flops | bytes accessed | tf_op | source)
XLA Modules:
  0.0 946.4 jit_solution(11480510170285200875)
XLA Ops:
  20.2 12.5 %copy.282 = f32[6,4,4,8,384]{3,2,4,1,0:T(4,128)} copy(f32[6,4,4,8,384]{4,3,2,1,0:T(8,128)S(1)} %fusion.109) | data formatting | bytes 2359296 | tf_op jit(solution)/shard_map/while/body/eval_jaxpr/slice | solution.py:84
  32.7 18.3 %copy.283 = f32[6,4,4,8,128,3]{4,5,3,2,1,0:T(4,128)S(1)} copy(f32[6,4,4,8,128,3]{3,2,5,4,1,0:T(4,128)} %bitcast.311) | data formatting | bytes 2359296 | tf_op jit(solution)/shard_map/while/body/eval_jaxpr/reshape | solution.py:84
  51.0 15.0 %slice.434 = f32[6,4,4,8,128]{4,3,2,1,0:T(8,128)S(1)} slice(f32[6,4,4,8,385]{4,3,2,1,0:T(8,128)} %pad_maximum_fusion.3), slice={[0:6:1], [0:4:1], [0:4:1], [0:8:1], [3:385:3]} | slice | bytes 786432 | tf_op jit(solution)/shard_map/while/body/eval_jaxpr/slice | solution.py:88
  119.8 10.7 %copy_bitcast_fusion = (f32[6,6,6,6,8,128]{5,4,3,2,1,0:T(8,128)}, f32[6,6,6,6,8,128]{5,4,3,2,1,0:T(8,128)}) fusion(f32[6,6,6,8,128,6]{4,5,3,2,1,0:T(8,128)} %fusion.16, f32[6,6,6,8,128,6]{4,5,3,2,1,0:T(8,128)} %fusion.18), kind=kLoop, calls=%fused_computation.12 | loop fusion | bytes 21233664 | tf_op jit(solution)/shard_map/while/body/eval_jaxpr/qa,cabgjk->cqbgjk/transpose | solution.py:69
  144.1 11.7 %add_bitcast_fusion = (f32[6,6,6,8,128]{4,3,2,1,0:T(8,128)}, f32[1,6,6,6,8,128]{5,4,3,2,1,0:T(8,128)}, f32[1,6,6,6,8,128]{5,4,3,2,1,0:T(8,128)}, f32[1,6,6,6,8,1...) fusion(f32[1,6,6,6,8,128]{5,4,3,2,1,0:T(8,128)} %get-tuple-elem, ...), kind=kLoop, calls=%fused_computation.143 | loop fusion | flops 25878528 | bytes 31850496 | tf_op jit(solution)/shard_map/reshape.83
  200.5 10.8 %fusion = f32[3,4,4,8,385]{3,2,4,1,0:T(4,128)} fusion(f32[3,4,4,8,384]{3,2,4,1,0:T(4,128)} %bitcast.323, f32[3,4,4,8,384]{3,2,4,1,0:T(4,128)S(1)} %bitcast.319), kind=kLoop, calls=%fused_computation.4 | loop fusion | flops 147840 | bytes 1771008 | tf_op jit(solution)/shard_map/while/body/eval_jaxpr/add | solution.py:111
  272.9 10.3 %copy.315 = f32[3,4,4,8,128,3]{4,5,3,2,1,0:T(4,128)} copy(f32[3,4,4,8,128,3]{3,2,5,4,1,0:T(4,128)} %bitcast.327) | data formatting | bytes 1179648 | tf_op jit(solution)/shard_map/while/body/eval_jaxpr/reshape | solution.py:84
  331.0 12.8 %fusion.1 = f32[3,4,4,8,385]{3,2,4,1,0:T(4,128)} fusion(f32[3,4,4,8,384]{3,2,4,1,0:T(4,128)} %bitcast.320, f32[3,4,4,8,384]{3,2,4,1,0:T(4,128)} %bitcast.324), kind=kLoop, calls=%fused_computation.5 | loop fusion | flops 147840 | bytes 1771008 | tf_op jit(solution)/shard_map/while/body/eval_jaxpr/add | solution.py:111
  359.3 10.0 %copy.324 = f32[3,4,8,3,385]{4,1,3,2,0:T(4,128)} copy(f32[3,4,8,3,385]{2,3,4,1,0:T(4,128)} %slice_bitcast_fusion.2) | data formatting | bytes 887040 | tf_op jit(solution)/shard_map/while/body/eval_jaxpr/transpose | solution.py:96
  391.0 30.6 %all-reduce.36 = (f32[]{:T(128)}, f32[]{:T(128)}) all-reduce(f32[]{:T(128)} %get-tuple-element.88, f32[]{:T(128)} %get-tuple-element.87), channel_id=1, replica_groups=mesh['gx'=8,'gy'=16] {'gy'}, use_global_device_ids=true, to_apply=%region_1.2 | all-reduce | flops 2 | bytes 16 | tf_op jit(solution)/shard_map/psum | solution.py:267
  421.6 23.9 %all-reduce.37 = (f32[]{:T(128)}, f32[]{:T(128)}) all-reduce(f32[]{:T(128)} %get-tuple-element.89, f32[]{:T(128)} %get-tuple-element.90), channel_id=1, replica_groups=mesh['gx'=8,'gy'=16] {'gx'}, use_global_device_ids=true, to_apply=%region_2.3 | all-reduce | flops 2 | bytes 16 | tf_op jit(solution)/shard_map/psum | solution.py:267
  448.5 29.5 %psum.88 = f32[]{:T(128)} all-reduce(f32[]{:T(128)} %get-tuple-element.116), channel_id=1, replica_groups=mesh['gx'=8,'gy'=16] {'gy'}, use_global_device_ids=true, to_apply=%region_7.8 | all-reduce | flops 1 | bytes 8 | tf_op jit(solution)/shard_map/psum | solution.py:267
  478.0 20.1 %psum.89 = f32[]{:T(128)} all-reduce(f32[]{:T(128)} %psum.88), channel_id=1, replica_groups=mesh['gx'=8,'gy'=16] {'gx'}, use_global_device_ids=true, to_apply=%region_8.9 | all-reduce | flops 1 | bytes 8 | tf_op jit(solution)/shard_map/psum | solution.py:267
  522.6 10.3 %copy.333 = f32[3,4,4,8,128,3]{4,5,3,2,1,0:T(4,128)} copy(f32[3,4,4,8,128,3]{3,2,5,4,1,0:T(4,128)} %bitcast.328) | data formatting | bytes 1179648 | tf_op jit(solution)/shard_map/while/body/eval_jaxpr/reshape | solution.py:84
  583.0 12.8 %fusion.2 = f32[3,4,4,8,385]{3,2,4,1,0:T(4,128)} fusion(f32[3,4,4,8,384]{3,2,4,1,0:T(4,128)} %bitcast.321, f32[3,4,4,8,384]{3,2,4,1,0:T(4,128)} %bitcast.325), kind=kLoop, calls=%fused_computation.6 | loop fusion | flops 147840 | bytes 1771008 | tf_op jit(solution)/shard_map/while/body/eval_jaxpr/add | solution.py:111
  611.3 10.0 %copy.341 = f32[3,4,8,3,385]{4,1,3,2,0:T(4,128)} copy(f32[3,4,8,3,385]{2,3,4,1,0:T(4,128)} %slice_bitcast_fusion.1) | data formatting | bytes 887040 | tf_op jit(solution)/shard_map/while/body/eval_jaxpr/transpose | solution.py:96
  644.4 30.3 %psum.90 = f32[]{:T(128)} all-reduce(f32[]{:T(128)} %get-tuple-element.114), channel_id=1, replica_groups=mesh['gx'=8,'gy'=16] {'gy'}, use_global_device_ids=true, to_apply=%region_10.11 | all-reduce | flops 1 | bytes 8 | tf_op jit(solution)/shard_map/psum | solution.py:267
  674.7 22.2 %psum.91 = f32[]{:T(128)} all-reduce(f32[]{:T(128)} %psum.90), channel_id=1, replica_groups=mesh['gx'=8,'gy'=16] {'gx'}, use_global_device_ids=true, to_apply=%region_11.12 | all-reduce | flops 1 | bytes 8 | tf_op jit(solution)/shard_map/psum | solution.py:267
  701.9 29.5 %psum.92 = f32[]{:T(128)} all-reduce(f32[]{:T(128)} %multiply_reduce_fusion), channel_id=1, replica_groups=mesh['gx'=8,'gy'=16] {'gy'}, use_global_device_ids=true, to_apply=%region_13.14 | all-reduce | flops 1 | bytes 8 | tf_op jit(solution)/shard_map/psum | solution.py:267
  734.0 20.1 %psum.93 = f32[]{:T(128)} all-reduce(f32[]{:T(128)} %psum.92), channel_id=1, replica_groups=mesh['gx'=8,'gy'=16] {'gx'}, use_global_device_ids=true, to_apply=%region_14.15 | all-reduce | flops 1 | bytes 8 | tf_op jit(solution)/shard_map/psum | solution.py:267
  777.2 10.3 %copy.350 = f32[3,4,4,8,128,3]{4,5,3,2,1,0:T(4,128)} copy(f32[3,4,4,8,128,3]{3,2,5,4,1,0:T(4,128)} %bitcast.329) | data formatting | bytes 1179648 | tf_op jit(solution)/shard_map/while/body/eval_jaxpr/reshape | solution.py:84
  833.1 12.8 %fusion.3 = f32[3,4,4,8,385]{3,2,4,1,0:T(4,128)} fusion(f32[3,4,4,8,384]{3,2,4,1,0:T(4,128)} %bitcast.322, f32[3,4,4,8,384]{3,2,4,1,0:T(4,128)} %bitcast.326), kind=kLoop, calls=%fused_computation.7 | loop fusion | flops 147840 | bytes 1771008 | tf_op jit(solution)/shard_map/while/body/eval_jaxpr/add | solution.py:111
  890.6 30.3 %psum.94 = f32[]{:T(128)} all-reduce(f32[]{:T(128)} %fusion.140), channel_id=1, replica_groups=mesh['gx'=8,'gy'=16] {'gy'}, use_global_device_ids=true, to_apply=%region_16.17 | all-reduce | flops 1 | bytes 8 | tf_op jit(solution)/shard_map/psum | solution.py:267
  921.6 22.2 %psum.95 = f32[]{:T(128)} all-reduce(f32[]{:T(128)} %psum.94), channel_id=1, replica_groups=mesh['gx'=8,'gy'=16] {'gx'}, use_global_device_ids=true, to_apply=%region_17.18 | all-reduce | flops 1 | bytes 8 | tf_op jit(solution)/shard_map/psum | solution.py:267
  (306 shorter events, 510.5 us)
Async XLA Ops:
  0.6 13.7 %copy-start.29 = (f32[6,3,1,1,1]{0,1,4,3,2:T(4,128)S(1)}, f32[6,3,1,1,1]{0,1,4,3,2:T(4,128)}, u32[]{:S(2)}) copy-start(f32[6,3,1,1,1]{0,1,4,3,2:T(4,128)} %constant.174) | copy-start | bytes 220
  2.7 6.7 collective-permute-start
  9.4 7.5 collective-permute-start.1
  32.7 33.3 %copy-start.22 = (f32[6,4,1,1,1,1]{0,1,5,4,3,2:T(4,128)S(1)}, f32[6,4,1,1,1,1]{0,1,5,4,3,2:T(4,128)}, u32[]{:S(2)}) copy-start(f32[6,4,1,1,1,1]{0,1,5,4,3,2:T(4,128)} %constant.172) | copy-start | bytes 292
  239.0 17.1 %copy-start.3 = (f32[216,1,8,128]{3,2,1,0:T(8,128)S(1)}, f32[216,1,8,128]{3,2,1,0:T(8,128)}, u32[]{:S(2)}) copy-start(f32[216,1,8,128]{3,2,1,0:T(8,128)} %param.11) | copy-start | bytes 2654212
  239.0 6.0 collective-permute-start.2
  245.1 4.1 collective-permute-start.3
  249.2 5.5 collective-permute-start.4
  254.8 2.7 collective-permute-start.5
  379.6 6.0 collective-permute-start.6
  385.7 4.5 collective-permute-start.7
  390.2 55.3 %copy-start.26 = (f32[3,1,24,384]{3,2,1,0:T(8,128)}, f32[3,1,24,384]{3,2,1,0:T(8,128)S(1)}, u32[]{:S(2)}) copy-start(f32[3,1,24,384]{3,2,1,0:T(8,128)S(1)} %maximum_add_fusion.2) | copy-start | bytes 331780
  499.6 4.2 collective-permute-start.8
  503.8 2.7 collective-permute-start.9
  632.9 67.0 %copy-start.30 = (f32[6,3,1,1,1]{0,1,4,3,2:T(4,128)S(1)}, f32[6,3,1,1,1]{0,1,4,3,2:T(4,128)}, u32[]{:S(2)}) copy-start(f32[6,3,1,1,1]{0,1,4,3,2:T(4,128)} %constant.174) | copy-start | bytes 220
  632.9 6.0 collective-permute-start.10
  639.0 4.0 collective-permute-start.11
  756.6 4.2 collective-permute-start.12
  760.8 2.8 collective-permute-start.13
  879.9 6.0 collective-permute-start.14
  881.5 39.4 %copy-start.27 = (f32[27,1,8,128]{3,2,1,0:T(8,128)S(1)}, f32[27,1,8,128]{3,2,1,0:T(8,128)}, u32[]{:S(2)}) copy-start(f32[27,1,8,128]{3,2,1,0:T(8,128)} %param.10) | copy-start | bytes 331780
  881.5 63.6 %copy-start.23 = (f32[3,3,24,384]{3,2,1,0:T(8,128)S(1)}, f32[3,3,24,384]{3,2,1,0:T(8,128)}, u32[]{:S(2)}) copy-start(f32[3,3,24,384]{3,2,1,0:T(8,128)} %param.8) | copy-start | bytes 995332
  881.5 63.6 %copy-start.24 = (f32[3,3,24,384]{3,2,1,0:T(8,128)S(1)}, f32[3,3,24,384]{3,2,1,0:T(8,128)}, u32[]{:S(2)}) copy-start(f32[3,3,24,384]{3,2,1,0:T(8,128)} %param.9) | copy-start | bytes 995332
  886.0 3.9 collective-permute-start.15
  (28 other events, 116.4 us)
